TPU v7x, 512 devices: a whole 4x8x8 slice. The times are simulated.
512 devices in a mesh: col: 64 (over y, z_lo, core), row: 8 (over x, z_hi).
Axes of the slice: x: 4, y: 8, z: 8 (z_hi: 2, z_lo: 4; z = z_hi * 4 + z_lo), core: 2. Of those that a mesh axis runs over, the one named last changes fastest.
Arguments:
- field: bfloat16 [128, 1024, 128], P('row', 'col'), may hold values from -6 to 6
- cotangent: bfloat16 [128, 1024, 128], P('row', 'col'), may hold values from -6 to 6
- w_first: bfloat16 [3, 3, 128, 128], replicated, may hold values from -0.1875 to 0.1875
- w_down: bfloat16 [3, 3, 128, 256], replicated, may hold values from -0.1875 to 0.1875
- w_up: bfloat16 [2, 2, 256, 128], replicated, may hold values from -0.375 to 0.375
- offsets: int32 [8, 64, 2], replicated, may hold values from -8 to 8
- blend_table: int32 [32, 32], replicated, may hold values from 1 to 16
Outputs:
- blended: bfloat16 [128, 1024, 128], P('row', 'col')
- field_grad: float32 [128, 1024, 128], P('row', 'col')
- grad_first: float32 [3, 3, 128, 128], replicated
- grad_down: float32 [3, 3, 128, 256], replicated
- grad_up: float32 [2, 2, 256, 128], replicated
Inputs may be any that keep to these rules, and one draw needn't show every extreme that they name: `offsets`: A patch's first cell lies 8 cells minus its offset before its tile's first cell on each axis.
All inputs are finite; a program needn't handle non-finite values.
Results may differ from a plain program's by a relative error of at most 0.015.
Values may be sent and summed in bfloat16 or wider, within the bound.
No kernel may reach another device: no remote copies, remote signals or barrier semaphores. Data moves between devices by JAX's collectives and lax.ppermute only.
A program may use at most 64 MiB of HBM per device.

v0:
```python
import math
import jax
import jax.numpy as jnp
from jax import lax
from jax.sharding import PartitionSpec as P

MARGIN = 8


def passed_along(block, axis, distance):
    devices = range(lax.axis_size(axis))
    route = [(i - distance, i) for i in devices if i - distance in devices]
    return lax.ppermute(block, axis, route)


def extended(x, sides, width):
    for axis, dim in sides:
        size, length = (lax.axis_size(axis), x.shape[dim])
        up = [(i, (i + 1) % size) for i in range(size - 1)]
        down = [(j, i) for i, j in up]
        last = lax.slice_in_dim(x, length - width, length, axis=dim)
        leading = lax.slice_in_dim(x, 0, width, axis=dim)
        before = lax.ppermute(last, axis, up)
        after = lax.ppermute(leading, axis, down)
        x = jnp.concatenate([before, x, after], axis=dim)
    return x


def conv_same(inputs, kernel):
    rows, cols, chans = inputs.shape
    padded = jnp.pad(inputs, ((1, 1), (1, 1), (0, 0)))
    total = jnp.zeros((rows * cols, kernel.shape[3]), jnp.float32)
    for row_tap in range(3):
        for col_tap in range(3):
            window = padded[row_tap : row_tap + rows, col_tap : col_tap + cols].reshape(
                rows * cols, chans
            )
            total = total + jnp.dot(
                window, kernel[row_tap, col_tap], preferred_element_type=jnp.float32
            )
    return total.reshape(rows, cols, kernel.shape[3])


def conv_down(inputs, kernel):
    rows, cols, chans = inputs.shape
    padded = jnp.pad(inputs, ((1, 1), (1, 1), (0, 0)))
    half_r = rows // 2
    half_c = cols // 2
    total = jnp.zeros((half_r * half_c, kernel.shape[3]), jnp.float32)
    for row_tap in range(3):
        for col_tap in range(3):
            window = padded[row_tap : row_tap + rows : 2, col_tap : col_tap + cols : 2].reshape(
                half_r * half_c, chans
            )
            total = total + jnp.dot(
                window, kernel[row_tap, col_tap], preferred_element_type=jnp.float32
            )
    return total.reshape(half_r, half_c, kernel.shape[3])


def conv_up(inputs, kernel):
    rows, cols, chans = inputs.shape
    flat = inputs.reshape(rows * cols, chans)
    lines = []
    for row_tap in range(2):
        pieces = []
        for col_tap in range(2):
            pieces.append(
                jnp.dot(flat, kernel[row_tap, col_tap], preferred_element_type=jnp.float32).reshape(
                    rows, cols, kernel.shape[3]
                )
            )
        lines.append(jnp.stack(pieces, axis=2))
    return jnp.stack(lines, axis=1).reshape(2 * rows, 2 * cols, kernel.shape[3])


def patch_net(patch, w_first, w_down, w_up):
    hidden = jax.nn.silu(conv_same(patch, w_first)).astype(jnp.bfloat16)
    lower = jax.nn.silu(conv_down(hidden, w_down)).astype(jnp.bfloat16)
    return hidden.astype(jnp.float32) + conv_up(lower, w_up)


def return_margins(canvas, tile_h, tile_w, edge):
    summed = canvas
    for heading in (1, -1):
        strip = canvas[tile_h + edge :] if heading == 1 else canvas[:edge]
        arrived = passed_along(strip.astype(jnp.bfloat16), "row", heading).astype(strip.dtype)
        if heading == 1:
            summed = summed.at[edge : 2 * edge].add(arrived)
        else:
            summed = summed.at[tile_h : tile_h + edge].add(arrived)
    middle = summed[edge : tile_h + edge]
    result = middle
    for heading in (1, -1):
        strip = middle[:, tile_w + edge :] if heading == 1 else middle[:, :edge]
        arrived = passed_along(strip.astype(jnp.bfloat16), "col", heading).astype(strip.dtype)
        if heading == 1:
            result = result.at[:, edge : 2 * edge].add(arrived)
        else:
            result = result.at[:, tile_w : tile_w + edge].add(arrived)
    return result[:, edge : tile_w + edge]


def weight_total(offsets, table_f, row_at, col_at, rows_n, cols_n, tile_h, tile_w, lead, reach):
    patch_h, patch_w = table_f.shape
    total = jnp.zeros((tile_h + 2 * lead, tile_w + 2 * lead), jnp.float32)
    for row_step in range(-reach, reach + 1):
        for col_step in range(-reach, reach + 1):
            near_row = row_at + row_step
            near_col = col_at + col_step
            inside = (
                (near_row >= 0) & (near_row < rows_n) & (near_col >= 0) & (near_col < cols_n)
            ).astype(jnp.float32)
            shift_pair = offsets[
                jnp.clip(near_row, 0, rows_n - 1), jnp.clip(near_col, 0, cols_n - 1)
            ]
            top = row_step * tile_h - MARGIN + shift_pair[0] + lead
            left = col_step * tile_w - MARGIN + shift_pair[1] + lead
            pick_rows = (
                jnp.arange(tile_h + 2 * lead)[:, None] - top == jnp.arange(patch_h)[None, :]
            ).astype(jnp.float32)
            pick_cols = (
                jnp.arange(tile_w + 2 * lead)[:, None] - left == jnp.arange(patch_w)[None, :]
            ).astype(jnp.float32)
            placed = jnp.dot(
                jnp.dot(pick_rows, table_f, precision=lax.Precision.HIGHEST),
                pick_cols.T,
                precision=lax.Precision.HIGHEST,
            )
            total = total + inside * placed
    return total


def per_device(field, cotangent, w_first, w_down, w_up, offsets, blend_table):
    tile_h, tile_w, chans = field.shape
    patch_h, patch_w = blend_table.shape
    edge = 2 * MARGIN
    rows_n = lax.axis_size("row")
    cols_n = lax.axis_size("col")
    row_at = lax.axis_index("row")
    col_at = lax.axis_index("col")
    table_f = blend_table.astype(jnp.float32)
    grown = extended(field, (("row", 0), ("col", 1)), edge)
    own_shift = offsets[row_at, col_at]
    start_r = MARGIN + own_shift[0]
    start_c = MARGIN + own_shift[1]
    zero = jnp.int32(0)
    patch = lax.dynamic_slice(grown, (start_r, start_c, zero), (patch_h, patch_w, chans))
    out_patch, back = jax.vjp(patch_net, patch, w_first, w_down, w_up)
    empty = jnp.zeros((tile_h + 2 * edge, tile_w + 2 * edge, chans), jnp.float32)
    canvas = lax.dynamic_update_slice(
        empty, table_f[:, :, None] * out_patch, (start_r, start_c, zero)
    )
    numer = return_margins(canvas, tile_h, tile_w, edge)
    weight_sum = weight_total(
        offsets, table_f, row_at, col_at, rows_n, cols_n, tile_h, tile_w, 0, 1
    )
    ratio = cotangent.astype(jnp.float32) / weight_sum[:, :, None]
    ratio_grown = extended(ratio.astype(jnp.bfloat16), (("row", 0), ("col", 1)), edge).astype(
        ratio.dtype
    )
    blended = (numer / weight_sum[:, :, None]).astype(jnp.bfloat16)
    out_grad = table_f[:, :, None] * lax.dynamic_slice(
        ratio_grown, (start_r, start_c, zero), (patch_h, patch_w, chans)
    )
    d_patch, d_first, d_down, d_up = back(out_grad)
    d_canvas = lax.dynamic_update_slice(
        empty, d_patch.astype(jnp.float32), (start_r, start_c, zero)
    )
    field_grad = return_margins(d_canvas, tile_h, tile_w, edge)
    g_first, g_down, g_up = lax.psum(
        (d_first.astype(jnp.float32), d_down.astype(jnp.float32), d_up.astype(jnp.float32)),
        ("col", "row"),
    )
    scale = 1.0 / math.sqrt(tile_h * rows_n * tile_w * cols_n)
    return (blended, field_grad, g_first * scale, g_down * scale, g_up * scale)


def solution(mesh):
    return jax.shard_map(
        per_device,
        mesh=mesh,
        in_specs=(P("row", "col", None), P("row", "col", None), P(), P(), P(), P(), P()),
        out_specs=(P("row", "col", None), P("row", "col", None), P(), P(), P()),
        check_vma=False,
    )
```

profile of v0, /device:TPU:17, one launch (start us, length us, event | category | flops | bytes accessed | tf_op | source)
XLA Modules:
  0.0 498.5 jit_solution(4310469566527345241)
XLA Ops:
  7.2 10.6 %collective-permute-start = (bf16[16,16,128]{2,1,0:T(8,128)(2,1)}, bf16[16,16,128]{2,1,0:T(8,128)(2,1)S(1)}, u32[]{:S(2)}, u32[]{:S(2)}) collective-permute-start(bf16[16,16,128]{2,1,0:T(8,128)(2,1)} %param.23), channel_id=1, source_target_pairs={{0,1},{1,2},{2,3},{3,4},{4,5},{5,6},{6,7},{8,9},{9,10},{10,11},{11... | collective-permute-start | bytes 196616 | tf_op jit(solution)/shard_map/ppermute | solution.py:23
  17.9 1.3 collective-permute-start.1
  19.2 1.0 constant_dynamic-slice_fusion
  23.4 0.9 fusion.167
  24.3 0.9 fusion.168
  26.5 0.9 fusion.169
  29.4 0.9 fusion.170
  31.7 0.9 fusion.171
  34.5 0.9 fusion.172
  36.8 0.9 fusion.173
  39.6 0.9 fusion.174
  41.9 0.9 fusion.175
  45.4 3.9 collective-permute-start.2
  49.3 1.9 collective-permute-start.3
  51.4 8.1 %collective-permute-start.8 = (bf16[16,16,128]{2,1,0:T(8,128)(2,1)S(1)}, bf16[16,16,128]{2,1,0:T(8,128)(2,1)S(1)}, u32[]{:S(2)}, u32[]{:S(2)}) collective-permute-start(bf16[16,16,128]{2,1,0:T(8,128)(2,1)S(1)} %divide_convert_fusion), channel_id=1, source_target_pairs={{0,1},{1,2},{2,3},{3,4},{4,5},{5,6},{6,7},{8,9},{9,10},{10,11},{11... | collective-permute-start | bytes 196616 | tf_op jit(solution)/shard_map/ppermute | solution.py:23
  59.5 1.3 collective-permute-start.9
  63.4 5.0 %collective-permute-done.9 = bf16[16,16,128]{2,1,0:T(8,128)(2,1)S(1)} collective-permute-done((bf16[16,16,128]{2,1,0:T(8,128)(2,1)S(1)}, bf16[16,16,128]{2,1,0:T(8,128)(2,1)S(1)}, u32[]{:S(2)}, u32[]{:S(2)}) %collective-permute-start.9) | collective-permute-done | bytes 65568 | tf_op jit(solution)/shard_map/ppermute | solution.py:24
  69.2 5.7 %collective-permute-start.10 = (bf16[48,16,128]{2,1,0:T(8,128)(2,1)}, bf16[48,16,128]{2,1,0:T(8,128)(2,1)}, u32[]{:S(2)}, u32[]{:S(2)}) collective-permute-start(bf16[48,16,128]{2,1,0:T(8,128)(2,1)} %pad_maximum_fusion.1), channel_id=1, source_target_pairs={{0,8},{8,16},{16,24},{24,32},{32,40},{40,48},{48,56},{56,64},{64,7... | collective-permute-start | bytes 589832 | tf_op jit(solution)/shard_map/ppermute | solution.py:23
  74.9 2.8 collective-permute-start.11
  88.6 2.3 convert_multiply_fusion.2
  107.4 5.6 %pad.156 = bf16[34,34,128]{2,1,0:T(8,128)(2,1)S(1)} pad(bf16[16,16,128]{2,1,0:T(8,128)(2,1)} %bitcast.505, bf16[]{:T(256)} %constant.241.clone.1), padding=2_1_1x0_3_1x0_0_0 | pad | bytes 361474 | tf_op jit(solution)/shard_map/transpose(jvp())/pad | solution.py:52
  113.0 8.5 %pad.345 = bf16[33,33,128]{2,1,0:T(8,128)(2,1)} pad(bf16[16,16,128]{2,1,0:T(8,128)(2,1)} %bitcast.504, bf16[]{:T(256)} %constant.241.clone.1), padding=0_2_1x0_2_1x0_0_0 | pad | bytes 344322
  121.5 8.5 %pad.348 = bf16[32,33,128]{2,1,0:T(8,128)(2,1)} pad(bf16[16,16,128]{2,1,0:T(8,128)(2,1)} %bitcast.511, bf16[]{:T(256)} %constant.241.clone.1), padding=0_1_1x0_2_1x0_0_0 | pad | bytes 335874
  130.0 8.4 %pad.346 = bf16[33,32,128]{2,1,0:T(8,128)(2,1)} pad(bf16[16,16,128]{2,1,0:T(8,128)(2,1)} %bitcast.510, bf16[]{:T(256)} %constant.241.clone.1), padding=0_2_1x0_1_1x0_0_0 | pad | bytes 335874
  138.4 8.4 %pad.347 = bf16[33,32,128]{2,1,0:T(8,128)(2,1)} pad(bf16[16,16,128]{2,1,0:T(8,128)(2,1)} %bitcast.509, bf16[]{:T(256)} %constant.241.clone.1), padding=0_2_1x1_0_1x0_0_0 | pad | bytes 335874
  146.8 8.4 %pad.214 = bf16[32,32,128]{2,1,0:T(8,128)(2,1)} pad(bf16[16,16,128]{2,1,0:T(8,128)(2,1)} %bitcast.503, bf16[]{:T(256)} %constant.241.clone.1), padding=0_1_1x1_0_1x0_0_0 | pad | bytes 327682 | tf_op jit(solution)/shard_map/transpose(jvp(jit(_pad)))/pad | solution.py:46
  155.2 5.6 %pad.215 = bf16[32,32,128]{2,1,0:T(8,128)(2,1)} pad(bf16[16,16,128]{2,1,0:T(8,128)(2,1)S(1)} %bitcast.502, bf16[]{:T(256)} %constant.241.clone.1), padding=0_1_1x0_1_1x0_0_0 | pad | bytes 327682 | tf_op jit(solution)/shard_map/transpose(jvp(jit(_pad)))/pad | solution.py:46
  162.0 1.7 fusion.52
  164.5 0.9 fusion.38
  166.3 0.9 fusion.40
  167.2 0.9 fusion.41
  172.8 1.3 dynamic_update_slice.7
  174.9 4.2 collective-permute-start.12
  179.1 1.3 collective-permute-start.13
  180.4 1.3 dynamic_update_slice.6
  182.7 8.6 %collective-permute-start.4 = (bf16[16,48,128]{2,1,0:T(8,128)(2,1)}, bf16[16,48,128]{2,1,0:T(8,128)(2,1)}, u32[]{:S(2)}, u32[]{:S(2)}) collective-permute-start(bf16[16,48,128]{2,1,0:T(8,128)(2,1)} %get-tuple-element.110), channel_id=1, source_target_pairs={{0,1},{1,2},{2,3},{3,4},{4,5},{5,6},{6,7},{8,9},{9,10},{10,11},{11... | collective-permute-start | bytes 589832 | tf_op jit(solution)/shard_map/ppermute | solution.py:13
  191.2 1.3 collective-permute-start.5
  194.6 1.2 add_convert_fusion
  195.8 11.9 %collective-permute-done.5 = bf16[16,48,128]{2,1,0:T(8,128)(2,1)} collective-permute-done((bf16[16,48,128]{2,1,0:T(8,128)(2,1)S(1)}, bf16[16,48,128]{2,1,0:T(8,128)(2,1)}, u32[]{:S(2)}, u32[]{:S(2)}) %collective-permute-start.5) | collective-permute-done | bytes 196640 | tf_op jit(solution)/shard_map/ppermute | solution.py:13
  207.6 1.1 fusion.205
  208.7 12.5 %collective-permute-start.6 = (bf16[16,16,128]{2,1,0:T(8,128)(2,1)S(1)}, bf16[16,16,128]{2,1,0:T(8,128)(2,1)S(1)}, u32[]{:S(2)}, u32[]{:S(2)}) collective-permute-start(bf16[16,16,128]{2,1,0:T(8,128)(2,1)S(1)} %get-tuple-element.128), channel_id=1, source_target_pairs={{0,8},{8,16},{16,24},{24,32},{32,40},{40,48},{48,56},{56,64},{64,7... | collective-permute-start | bytes 196616 | tf_op jit(solution)/shard_map/ppermute | solution.py:13
  221.3 1.9 collective-permute-start.7
  223.2 1.1 fusion.203
  224.3 3.6 collective-permute-start.14
  228.0 1.9 collective-permute-start.15
  230.7 3.3 collective-permute-done.15
  234.7 252.5 %all-reduce.45.cloned.1.call-done = (f32[3,3,128,128]{3,2,1,0:T(8,128)}, f32[3,3,128,256]{3,2,1,0:T(8,128)}, f32[2,2,256,128]{3,2,1,0:T(8,128)}) async-done(((f32[3,3,128,128]{3,2,1,0:T(8,128)}, f32[3,3,128,256]{3,2,1,0:T(8,128)}, f32[2,2,256,128]{3,2,1,0:T(8,128)}), (f32[3,3,128,128]{3,2,1,0:T(8,128)}, f32[3,3,128,256]{3,2,1,0:T(8,128)}, f32[2,2,256,128]{3,2,1,0:T(8,128)})) %all-reduce.45.cloned.1.call-update) | async-done | bytes 2293776 | tf_op jit(solution)/shard_map/psum | solution.py:171
  487.1 2.4 broadcast_multiply_fusion
  (244 shorter events, 47.3 us)
Async XLA Ops:
  7.2 38.1 %copy-start.35 = (bf16[16,16,128]{2,1,0:T(8,128)(2,1)S(1)}, bf16[16,16,128]{2,1,0:T(8,128)(2,1)}, u32[]{:S(2)}) copy-start(bf16[16,16,128]{2,1,0:T(8,128)(2,1)} %param.23) | copy-start | bytes 196612
  7.2 56.2 %copy-start.43 = (s32[32,32]{1,0:T(8,128)S(1)}, s32[32,32]{1,0:T(8,128)}, u32[]{:S(2)}) copy-start(s32[32,32]{1,0:T(8,128)} %param.29) | copy-start | bytes 12292
  7.2 44.1 %copy-start.36 = (bf16[16,16,128]{2,1,0:T(8,128)(2,1)S(1)}, bf16[16,16,128]{2,1,0:T(8,128)(2,1)}, u32[]{:S(2)}) copy-start(bf16[16,16,128]{2,1,0:T(8,128)(2,1)} %param.24) | copy-start | bytes 196612
  7.2 479.9 %all-reduce.45.cloned.1.call-start = ((), (), s32[]{:S(2)}) async-start(), calls=%async_computation | async-start | bytes 4587520 | tf_op jit(solution)/shard_map/psum | solution.py:171
  7.2 38.0 %collective-permute-start = (bf16[16,16,128]{2,1,0:T(8,128)(2,1)}, bf16[16,16,128]{2,1,0:T(8,128)(2,1)S(1)}, u32[]{:S(2)}, u32[]{:S(2)}) collective-permute-start(bf16[16,16,128]{2,1,0:T(8,128)(2,1)} %param.23), channel_id=1, source_target_pairs={{0,1},{1,2},{2,3},{3,4},{4,5},{5,6},{6,7},{8,9},{9,10},{10,11},{11... | collective-permute-start | bytes 196616 | tf_op jit(solution)/shard_map/ppermute | solution.py:23
  17.9 27.5 %collective-permute-start.1 = (bf16[16,16,128]{2,1,0:T(8,128)(2,1)}, bf16[16,16,128]{2,1,0:T(8,128)(2,1)S(1)}, u32[]{:S(2)}, u32[]{:S(2)}) collective-permute-start(bf16[16,16,128]{2,1,0:T(8,128)(2,1)} %param.23), channel_id=1, source_target_pairs={{1,0},{2,1},{3,2},{4,3},{5,4},{6,5},{7,6},{9,8},{10,9},{11,10},{12... | collective-permute-start | bytes 196616 | tf_op jit(solution)/shard_map/ppermute | solution.py:24
  45.4 32.4 %collective-permute-start.2 = (bf16[48,16,128]{2,1,0:T(8,128)(2,1)S(1)}, bf16[48,16,128]{2,1,0:T(8,128)(2,1)S(1)}, u32[]{:S(2)}, u32[]{:S(2)}) collective-permute-start(bf16[48,16,128]{2,1,0:T(8,128)(2,1)S(1)} %constant_dynamic-update-slice_fusion), channel_id=1, source_target_pairs={{0,8},{8,16},{16,24},{24,32},{32,40},{40,48},{48,56},{56,64},{64,7... | collective-permute-start | bytes 589832 | tf_op jit(solution)/shard_map/ppermute | solution.py:23
  49.3 28.4 %collective-permute-start.3 = (bf16[48,16,128]{2,1,0:T(8,128)(2,1)S(1)}, bf16[48,16,128]{2,1,0:T(8,128)(2,1)S(1)}, u32[]{:S(2)}, u32[]{:S(2)}) collective-permute-start(bf16[48,16,128]{2,1,0:T(8,128)(2,1)S(1)} %constant_dynamic-update-slice_fusion), channel_id=1, source_target_pairs={{8,0},{16,8},{24,16},{32,24},{40,32},{48,40},{56,48},{64,56},{72,6... | collective-permute-start | bytes 589832 | tf_op jit(solution)/shard_map/ppermute | solution.py:24
  51.4 12.0 %collective-permute-start.8 = (bf16[16,16,128]{2,1,0:T(8,128)(2,1)S(1)}, bf16[16,16,128]{2,1,0:T(8,128)(2,1)S(1)}, u32[]{:S(2)}, u32[]{:S(2)}) collective-permute-start(bf16[16,16,128]{2,1,0:T(8,128)(2,1)S(1)} %divide_convert_fusion), channel_id=1, source_target_pairs={{0,1},{1,2},{2,3},{3,4},{4,5},{5,6},{6,7},{8,9},{9,10},{10,11},{11... | collective-permute-start | bytes 196616 | tf_op jit(solution)/shard_map/ppermute | solution.py:23
  59.5 9.0 %collective-permute-start.9 = (bf16[16,16,128]{2,1,0:T(8,128)(2,1)S(1)}, bf16[16,16,128]{2,1,0:T(8,128)(2,1)S(1)}, u32[]{:S(2)}, u32[]{:S(2)}) collective-permute-start(bf16[16,16,128]{2,1,0:T(8,128)(2,1)S(1)} %divide_convert_fusion), channel_id=1, source_target_pairs={{1,0},{2,1},{3,2},{4,3},{5,4},{6,5},{7,6},{9,8},{10,9},{11,10},{12... | collective-permute-start | bytes 196616 | tf_op jit(solution)/shard_map/ppermute | solution.py:24
  63.4 14.9 %copy-start.29 = (bf16[16,16,128]{2,1,0:T(8,128)(2,1)}, bf16[16,16,128]{2,1,0:T(8,128)(2,1)S(1)}, u32[]{:S(2)}) copy-start(bf16[16,16,128]{2,1,0:T(8,128)(2,1)S(1)} %collective-permute-done.8) | copy-start | bytes 196612
  68.5 9.9 %copy-start.31 = (bf16[16,16,128]{2,1,0:T(8,128)(2,1)}, bf16[16,16,128]{2,1,0:T(8,128)(2,1)S(1)}, u32[]{:S(2)}) copy-start(bf16[16,16,128]{2,1,0:T(8,128)(2,1)S(1)} %collective-permute-done.9) | copy-start | bytes 196612
  69.2 19.0 %collective-permute-start.10 = (bf16[48,16,128]{2,1,0:T(8,128)(2,1)}, bf16[48,16,128]{2,1,0:T(8,128)(2,1)}, u32[]{:S(2)}, u32[]{:S(2)}) collective-permute-start(bf16[48,16,128]{2,1,0:T(8,128)(2,1)} %pad_maximum_fusion.1), channel_id=1, source_target_pairs={{0,8},{8,16},{16,24},{24,32},{32,40},{40,48},{48,56},{56,64},{64,7... | collective-permute-start | bytes 589832 | tf_op jit(solution)/shard_map/ppermute | solution.py:23
  74.9 13.3 %collective-permute-start.11 = (bf16[48,16,128]{2,1,0:T(8,128)(2,1)}, bf16[48,16,128]{2,1,0:T(8,128)(2,1)}, u32[]{:S(2)}, u32[]{:S(2)}) collective-permute-start(bf16[48,16,128]{2,1,0:T(8,128)(2,1)} %pad_maximum_fusion.1), channel_id=1, source_target_pairs={{8,0},{16,8},{24,16},{32,24},{40,32},{48,40},{56,48},{64,56},{72,6... | collective-permute-start | bytes 589832 | tf_op jit(solution)/shard_map/ppermute | solution.py:24
  80.9 4.0 copy-start
  81.7 3.7 copy-start.16
  83.3 2.3 copy-start.8
  83.7 2.1 copy-start.10
  84.1 1.9 copy-start.12
  95.4 2.5 copy-start.13
  95.4 3.3 copy-start.11
  95.6 3.9 copy-start.9
  174.9 48.3 %collective-permute-start.12 = (bf16[16,48,128]{2,1,0:T(8,128)(2,1)}, bf16[16,48,128]{2,1,0:T(8,128)(2,1)}, u32[]{:S(2)}, u32[]{:S(2)}) collective-permute-start(bf16[16,48,128]{2,1,0:T(8,128)(2,1)} %get-tuple-element.108), channel_id=1, source_target_pairs={{0,1},{1,2},{2,3},{3,4},{4,5},{5,6},{6,7},{8,9},{9,10},{10,11},{11... | collective-permute-start | bytes 589832 | tf_op jit(solution)/shard_map/ppermute | solution.py:13
  179.1 44.1 %collective-permute-start.13 = (bf16[16,48,128]{2,1,0:T(8,128)(2,1)S(1)}, bf16[16,48,128]{2,1,0:T(8,128)(2,1)}, u32[]{:S(2)}, u32[]{:S(2)}) collective-permute-start(bf16[16,48,128]{2,1,0:T(8,128)(2,1)S(1)} %get-tuple-element.109), channel_id=1, source_target_pairs={{1,0},{2,1},{3,2},{4,3},{5,4},{6,5},{7,6},{9,8},{10,9},{11,10},{12... | collective-permute-start | bytes 589832 | tf_op jit(solution)/shard_map/ppermute | solution.py:13
  181.7 10.8 %copy-start.25 = (bf16[1,1,256,128]{3,2,1,0:T(8,128)(2,1)S(1)}, bf16[1,1,256,128]{3,2,1,0:T(8,128)(2,1)}, u32[]{:S(2)}) copy-start(bf16[1,1,256,128]{3,2,1,0:T(8,128)(2,1)} %fusion.14) | copy-start | bytes 196612
  181.7 10.8 %copy-start.26 = (bf16[1,1,256,128]{3,2,1,0:T(8,128)(2,1)S(1)}, bf16[1,1,256,128]{3,2,1,0:T(8,128)(2,1)}, u32[]{:S(2)}) copy-start(bf16[1,1,256,128]{3,2,1,0:T(8,128)(2,1)} %fusion.13) | copy-start | bytes 196612
  181.7 10.8 %copy-start.27 = (bf16[1,1,256,128]{3,2,1,0:T(8,128)(2,1)S(1)}, bf16[1,1,256,128]{3,2,1,0:T(8,128)(2,1)}, u32[]{:S(2)}) copy-start(bf16[1,1,256,128]{3,2,1,0:T(8,128)(2,1)} %fusion.15) | copy-start | bytes 196612
  181.7 10.8 %copy-start.28 = (bf16[1,1,256,128]{3,2,1,0:T(8,128)(2,1)S(1)}, bf16[1,1,256,128]{3,2,1,0:T(8,128)(2,1)}, u32[]{:S(2)}) copy-start(bf16[1,1,256,128]{3,2,1,0:T(8,128)(2,1)} %fusion.16) | copy-start | bytes 196612
  181.8 11.5 %copy-start.37 = (bf16[1,1,128,128]{3,2,1,0:T(8,128)(2,1)S(1)}, bf16[1,1,128,128]{3,2,1,0:T(8,128)(2,1)}, u32[]{:S(2)}) copy-start(bf16[1,1,128,128]{3,2,1,0:T(8,128)(2,1)} %fusion.38) | copy-start | bytes 98308
  181.9 11.5 %copy-start.38 = (bf16[1,1,128,128]{3,2,1,0:T(8,128)(2,1)S(1)}, bf16[1,1,128,128]{3,2,1,0:T(8,128)(2,1)}, u32[]{:S(2)}) copy-start(bf16[1,1,128,128]{3,2,1,0:T(8,128)(2,1)} %fusion.39) | copy-start | bytes 98308
  181.9 11.5 %copy-start.39 = (bf16[1,1,128,128]{3,2,1,0:T(8,128)(2,1)S(1)}, bf16[1,1,128,128]{3,2,1,0:T(8,128)(2,1)}, u32[]{:S(2)}) copy-start(bf16[1,1,128,128]{3,2,1,0:T(8,128)(2,1)} %fusion.40) | copy-start | bytes 98308
  181.9 11.5 %copy-start.40 = (bf16[1,1,128,128]{3,2,1,0:T(8,128)(2,1)S(1)}, bf16[1,1,128,128]{3,2,1,0:T(8,128)(2,1)}, u32[]{:S(2)}) copy-start(bf16[1,1,128,128]{3,2,1,0:T(8,128)(2,1)} %fusion.41) | copy-start | bytes 98308
  181.9 11.5 %copy-start.41 = (bf16[1,1,128,128]{3,2,1,0:T(8,128)(2,1)S(1)}, bf16[1,1,128,128]{3,2,1,0:T(8,128)(2,1)}, u32[]{:S(2)}) copy-start(bf16[1,1,128,128]{3,2,1,0:T(8,128)(2,1)} %fusion.42) | copy-start | bytes 98308
  181.9 11.5 %copy-start.42 = (bf16[1,1,128,128]{3,2,1,0:T(8,128)(2,1)S(1)}, bf16[1,1,128,128]{3,2,1,0:T(8,128)(2,1)}, u32[]{:S(2)}) copy-start(bf16[1,1,128,128]{3,2,1,0:T(8,128)(2,1)} %fusion.43) | copy-start | bytes 98308
  181.9 12.4 %copy-start.17 = (bf16[16,16,128]{2,1,0:T(8,128)(2,1)S(1)}, bf16[16,16,128]{2,1,0:T(8,128)(2,1)}, u32[]{:S(2)}) copy-start(bf16[16,16,128]{2,1,0:T(8,128)(2,1)} %copy-done.16) | copy-start | bytes 196612
  181.9 12.6 %copy-start.19 = (bf16[1,1,128,256]{3,2,1,0:T(8,128)(2,1)S(1)}, bf16[1,1,128,256]{3,2,1,0:T(8,128)(2,1)}, u32[]{:S(2)}) copy-start(bf16[1,1,128,256]{3,2,1,0:T(8,128)(2,1)} %fusion.25) | copy-start | bytes 196612
  181.9 12.6 %copy-start.20 = (bf16[1,1,128,256]{3,2,1,0:T(8,128)(2,1)S(1)}, bf16[1,1,128,256]{3,2,1,0:T(8,128)(2,1)}, u32[]{:S(2)}) copy-start(bf16[1,1,128,256]{3,2,1,0:T(8,128)(2,1)} %fusion.24) | copy-start | bytes 196612
  181.9 12.6 %copy-start.21 = (bf16[1,1,128,256]{3,2,1,0:T(8,128)(2,1)S(1)}, bf16[1,1,128,256]{3,2,1,0:T(8,128)(2,1)}, u32[]{:S(2)}) copy-start(bf16[1,1,128,256]{3,2,1,0:T(8,128)(2,1)} %fusion.23) | copy-start | bytes 196612
  182.0 12.6 %copy-start.22 = (bf16[1,1,128,256]{3,2,1,0:T(8,128)(2,1)S(1)}, bf16[1,1,128,256]{3,2,1,0:T(8,128)(2,1)}, u32[]{:S(2)}) copy-start(bf16[1,1,128,256]{3,2,1,0:T(8,128)(2,1)} %fusion.22) | copy-start | bytes 196612
  182.0 12.6 %copy-start.23 = (bf16[1,1,128,256]{3,2,1,0:T(8,128)(2,1)S(1)}, bf16[1,1,128,256]{3,2,1,0:T(8,128)(2,1)}, u32[]{:S(2)}) copy-start(bf16[1,1,128,256]{3,2,1,0:T(8,128)(2,1)} %fusion.21) | copy-start | bytes 196612
  182.0 12.6 %copy-start.24 = (bf16[1,1,128,256]{3,2,1,0:T(8,128)(2,1)S(1)}, bf16[1,1,128,256]{3,2,1,0:T(8,128)(2,1)}, u32[]{:S(2)}) copy-start(bf16[1,1,128,256]{3,2,1,0:T(8,128)(2,1)} %fusion.20) | copy-start | bytes 196612
  182.7 13.1 %collective-permute-start.4 = (bf16[16,48,128]{2,1,0:T(8,128)(2,1)}, bf16[16,48,128]{2,1,0:T(8,128)(2,1)}, u32[]{:S(2)}, u32[]{:S(2)}) collective-permute-start(bf16[16,48,128]{2,1,0:T(8,128)(2,1)} %get-tuple-element.110), channel_id=1, source_target_pairs={{0,1},{1,2},{2,3},{3,4},{4,5},{5,6},{6,7},{8,9},{9,10},{10,11},{11... | collective-permute-start | bytes 589832 | tf_op jit(solution)/shard_map/ppermute | solution.py:13
  191.2 16.4 %collective-permute-start.5 = (bf16[16,48,128]{2,1,0:T(8,128)(2,1)S(1)}, bf16[16,48,128]{2,1,0:T(8,128)(2,1)}, u32[]{:S(2)}, u32[]{:S(2)}) collective-permute-start(bf16[16,48,128]{2,1,0:T(8,128)(2,1)S(1)} %get-tuple-element.111), channel_id=1, source_target_pairs={{1,0},{2,1},{3,2},{4,3},{5,4},{6,5},{7,6},{9,8},{10,9},{11,10},{12... | collective-permute-start | bytes 589832 | tf_op jit(solution)/shard_map/ppermute | solution.py:13
  208.7 21.2 %collective-permute-start.6 = (bf16[16,16,128]{2,1,0:T(8,128)(2,1)S(1)}, bf16[16,16,128]{2,1,0:T(8,128)(2,1)S(1)}, u32[]{:S(2)}, u32[]{:S(2)}) collective-permute-start(bf16[16,16,128]{2,1,0:T(8,128)(2,1)S(1)} %get-tuple-element.128), channel_id=1, source_target_pairs={{0,8},{8,16},{16,24},{24,32},{32,40},{40,48},{48,56},{56,64},{64,7... | collective-permute-start | bytes 196616 | tf_op jit(solution)/shard_map/ppermute | solution.py:13
  221.3 8.7 %collective-permute-start.7 = (bf16[16,16,128]{2,1,0:T(8,128)(2,1)S(1)}, bf16[16,16,128]{2,1,0:T(8,128)(2,1)S(1)}, u32[]{:S(2)}, u32[]{:S(2)}) collective-permute-start(bf16[16,16,128]{2,1,0:T(8,128)(2,1)S(1)} %get-tuple-element.129), channel_id=1, source_target_pairs={{8,0},{16,8},{24,16},{32,24},{40,32},{48,40},{56,48},{64,56},{72,6... | collective-permute-start | bytes 196616 | tf_op jit(solution)/shard_map/ppermute | solution.py:13
  224.3 6.3 %collective-permute-start.14 = (bf16[16,16,128]{2,1,0:T(8,128)(2,1)S(1)}, bf16[16,16,128]{2,1,0:T(8,128)(2,1)S(1)}, u32[]{:S(2)}, u32[]{:S(2)}) collective-permute-start(bf16[16,16,128]{2,1,0:T(8,128)(2,1)S(1)} %get-tuple-element.126), channel_id=1, source_target_pairs={{0,8},{8,16},{16,24},{24,32},{32,40},{40,48},{48,56},{56,64},{64,7... | collective-permute-start | bytes 196616 | tf_op jit(solution)/shard_map/ppermute | solution.py:13
  228.0 6.0 %collective-permute-start.15 = (bf16[16,16,128]{2,1,0:T(8,128)(2,1)S(1)}, bf16[16,16,128]{2,1,0:T(8,128)(2,1)S(1)}, u32[]{:S(2)}, u32[]{:S(2)}) collective-permute-start(bf16[16,16,128]{2,1,0:T(8,128)(2,1)S(1)} %get-tuple-element.127), channel_id=1, source_target_pairs={{8,0},{16,8},{24,16},{32,24},{40,32},{48,40},{56,48},{64,56},{72,6... | collective-permute-start | bytes 196616 | tf_op jit(solution)/shard_map/ppermute | solution.py:13
  487.1 2.5 copy-start.7
  (13 other events, 15.0 us)
Sparse Core Ops, SparseCore 0:
  195.9 291.1 all-reduce.44
where the time goes:
time: 502 us; the launch traced here: 499 us
  waiting for transfers between devices  273 us (54%)
  starting transfers between devices  71.1 us (14%)
  local copies, waits for them, and re-layouts  70.1 us (14%)
  matrix products  37.5 us (7%)
  between operations  30.1 us (6%)
  other arithmetic  17.1 us (3%)
    psum x1, waiting for transfers between devices, per_device(): lax.psum((d_first.astype(jnp.float32), d_down.astype(jnp.float32), d_up.a...  252 us
    unnamed x94, local copies, waits for them, and re-layouts  37.2 us
    ppermute x8, starting transfers between devices, passed_along(): return lax.ppermute(block, axis, route)  35.3 us
    ppermute x4, starting transfers between devices, extended(): before = lax.ppermute(last, axis, up)  28.4 us
    ppermute x8, waiting for transfers between devices, passed_along(): return lax.ppermute(block, axis, route)  15.2 us
    pad x3, local copies, waits for them, and re-layouts, conv_down(): padded = jnp.pad(inputs, ((1, 1), (1, 1), (0, 0)))  14.1 us
    dot_general x27, matrix products, conv_down(): jnp.dot(window, kernel[row_tap, col_tap], preferred_element_type=jnp.floa...  12.5 us
    dot_general x27, matrix products, conv_same(): jnp.dot(window, kernel[row_tap, col_tap], preferred_element_type=jnp.floa...  10.1 us
  transfers between devices with their start and end apart: 17, of which 4 were waited for; matrix products, arithmetic and copies ran while one was open for 7% of the time, Pallas kernels for 0%

commit v1 on v0

--- a/solution.py
+++ b/solution.py
@@ -5,6 +5,11 @@
 from jax.sharding import PartitionSpec as P
 
 MARGIN = 8
+
+
+def axis_by_axis(array, first, second):
+    inner = lax.psum(array, first)
+    return lax.psum(inner, second)
 
 
 def passed_along(block, axis, distance):
@@ -168,9 +173,10 @@
         empty, d_patch.astype(jnp.float32), (start_r, start_c, zero)
     )
     field_grad = return_margins(d_canvas, tile_h, tile_w, edge)
-    g_first, g_down, g_up = lax.psum(
+    g_first, g_down, g_up = axis_by_axis(
         (d_first.astype(jnp.float32), d_down.astype(jnp.float32), d_up.astype(jnp.float32)),
-        ("col", "row"),
+        "col",
+        "row",
     )
     scale = 1.0 / math.sqrt(tile_h * rows_n * tile_w * cols_n)
     return (blended, field_grad, g_first * scale, g_down * scale, g_up * scale)

time: 502 us -> 953 us (1.90)
  the two profiles are of different devices: /device:TPU:17 before, /device:TPU:129 now
where the time goes in v1:
time: 953 us; the launch traced here: 951 us
  waiting for transfers between devices  731 us (77%)
  starting transfers between devices  85.4 us (9%)
  local copies, waits for them, and re-layouts  54.5 us (6%)
  matrix products  33.8 us (4%)
  between operations  29.6 us (3%)
  other arithmetic  16.2 us (2%)
    psum x1, waiting for transfers between devices, axis_by_axis(): inner = lax.psum(array, first)  536 us
    psum x1, waiting for transfers between devices, axis_by_axis(): return lax.psum(inner, second)  162 us
    ppermute x8, starting transfers between devices, passed_along(): return lax.ppermute(block, axis, route)  54.7 us
    unnamed x82, local copies, waits for them, and re-layouts  31.7 us
    ppermute x8, waiting for transfers between devices, passed_along(): return lax.ppermute(block, axis, route)  26 us
    ppermute x4, starting transfers between devices, extended(): before = lax.ppermute(last, axis, up)  24 us
  transfers between devices with their start and end apart: 18, of which 6 were waited for; matrix products, arithmetic and copies ran while one was open for 3% of the time, Pallas kernels for 0%

profile of v1, /device:TPU:129, one launch (start us, length us, event | category | flops | bytes accessed | tf_op | source)
XLA Modules:
  0.0 950.7 jit_solution(1196048956024625136)
XLA Ops:
  7.2 8.8 collective-permute-start
  16.1 1.3 collective-permute-start.1
  17.4 1.0 constant_dynamic-slice_fusion
  21.5 0.9 fusion.167
  22.4 0.9 fusion.168
  24.6 0.9 fusion.169
  27.3 0.9 fusion.170
  29.5 0.9 fusion.171
  32.3 0.9 fusion.172
  34.4 0.9 fusion.173
  37.2 0.9 fusion.174
  39.4 0.9 fusion.175
  42.9 3.9 collective-permute-start.2
  46.8 1.9 collective-permute-start.3
  48.9 8.1 collective-permute-start.8
  57.0 1.3 collective-permute-start.9
  60.9 6.9 collective-permute-done.9
  68.5 3.1 collective-permute-start.10
  71.7 1.9 collective-permute-start.11
  84.3 2.3 convert_multiply_fusion.2
  102.9 5.6 pad.345
  108.5 8.5 pad.348
  117.0 8.4 pad.346
  125.4 5.6 pad.347
  131.0 5.6 pad.214
  136.6 5.6 pad.215
  142.2 0.9 copy-done.2
  143.3 1.8 fusion.52
  148.8 1.2 add_convert_fusion
  149.9 0.9 add_convert_fusion.1
  151.6 0.9 convolution_convert_fusion.6
  153.6 535.7 %all-reduce.47.cloned.1.call-done = (f32[3,3,128,128]{3,2,1,0:T(8,128)}, f32[3,3,128,256]{3,2,1,0:T(8,128)}, f32[2,2,256,128]{3,2,1,0:T(8,128)}) async-done(((f32[3,3,128,128]{3,2,1,0:T(8,128)}, f32[3,3,128,256]{3,2,1,0:T(8,128)}, f32[2,2,256,128]{3,2,1,0:T(8,128)}), (f32[3,3,128,128]{3,2,1,0:T(8,128)}, f32[3,3,128,256]{3,2,1,0:T(8,128)}, f32[2,2,256,128]{3,2,1,0:T(8,128)})) %all-reduce.47.cloned.1.call-update) | async-done | bytes 2293776 | tf_op jit(solution)/shard_map/psum | solution.py:11
  689.6 1.2 pad_add_fusion
  691.5 1.3 dynamic_update_slice.7
  692.9 1.3 dynamic_update_slice.6
  694.3 6.4 collective-permute-start.4
  700.7 1.3 collective-permute-start.5
  702.0 7.9 collective-permute-start.12
  710.0 1.3 collective-permute-start.13
  711.3 8.1 collective-permute-done.5
  719.5 1.9 collective-permute-start.6
  721.4 17.8 %collective-permute-start.7 = (bf16[16,16,128]{2,1,0:T(8,128)(2,1)S(1)}, bf16[16,16,128]{2,1,0:T(8,128)(2,1)S(1)}, u32[]{:S(2)}, u32[]{:S(2)}) collective-permute-start(bf16[16,16,128]{2,1,0:T(8,128)(2,1)S(1)} %get-tuple-element.132), channel_id=1, source_target_pairs={{8,0},{16,8},{24,16},{32,24},{40,32},{48,40},{56,48},{64,56},{72,6... | collective-permute-start | bytes 196616 | tf_op jit(solution)/shard_map/ppermute | solution.py:18
  739.3 17.8 %collective-permute-done.13 = bf16[16,48,128]{2,1,0:T(8,128)(2,1)S(1)} collective-permute-done((bf16[16,48,128]{2,1,0:T(8,128)(2,1)S(1)}, bf16[16,48,128]{2,1,0:T(8,128)(2,1)S(1)}, u32[]{:S(2)}, u32[]{:S(2)}) %collective-permute-start.13) | collective-permute-done | bytes 196640 | tf_op jit(solution)/shard_map/ppermute | solution.py:18
  757.1 1.9 collective-permute-start.14
  759.1 16.2 %collective-permute-start.15 = (bf16[16,16,128]{2,1,0:T(8,128)(2,1)S(1)}, bf16[16,16,128]{2,1,0:T(8,128)(2,1)S(1)}, u32[]{:S(2)}, u32[]{:S(2)}) collective-permute-start(bf16[16,16,128]{2,1,0:T(8,128)(2,1)S(1)} %get-tuple-element.130), channel_id=1, source_target_pairs={{8,0},{16,8},{24,16},{32,24},{40,32},{48,40},{56,48},{64,56},{72,6... | collective-permute-start | bytes 196616 | tf_op jit(solution)/shard_map/ppermute | solution.py:18
  776.8 162.5 %all-reduce.49.cloned.1.call-done = (f32[3,3,128,128]{3,2,1,0:T(8,128)}, f32[3,3,128,256]{3,2,1,0:T(8,128)}, f32[2,2,256,128]{3,2,1,0:T(8,128)}) async-done(((f32[3,3,128,128]{3,2,1,0:T(8,128)}, f32[3,3,128,256]{3,2,1,0:T(8,128)}, f32[2,2,256,128]{3,2,1,0:T(8,128)}), (f32[3,3,128,128]{3,2,1,0:T(8,128)}, f32[3,3,128,256]{3,2,1,0:T(8,128)}, f32[2,2,256,128]{3,2,1,0:T(8,128)})) %all-reduce.49.cloned.1.call-update) | async-done | bytes 2293776 | tf_op jit(solution)/shard_map/psum | solution.py:12
  939.3 2.4 broadcast_multiply_fusion
  941.8 0.9 broadcast_multiply_fusion.1
  (235 shorter events, 41.5 us)
Async XLA Ops:
  7.2 35.6 %copy-start.35 = (bf16[16,16,128]{2,1,0:T(8,128)(2,1)S(1)}, bf16[16,16,128]{2,1,0:T(8,128)(2,1)}, u32[]{:S(2)}) copy-start(bf16[16,16,128]{2,1,0:T(8,128)(2,1)} %param.23) | copy-start | bytes 196612
  7.2 53.7 %copy-start.37 = (s32[32,32]{1,0:T(8,128)S(1)}, s32[32,32]{1,0:T(8,128)}, u32[]{:S(2)}) copy-start(s32[32,32]{1,0:T(8,128)} %param.29) | copy-start | bytes 12292
  7.2 41.6 %copy-start.36 = (bf16[16,16,128]{2,1,0:T(8,128)(2,1)S(1)}, bf16[16,16,128]{2,1,0:T(8,128)(2,1)}, u32[]{:S(2)}) copy-start(bf16[16,16,128]{2,1,0:T(8,128)(2,1)} %param.24) | copy-start | bytes 196612
  7.2 682.2 %all-reduce.47.cloned.1.call-start = ((), (), s32[]{:S(2)}) async-start(), calls=%async_computation | async-start | bytes 4587520 | tf_op jit(solution)/shard_map/psum | solution.py:11
  7.2 35.5 %collective-permute-start = (bf16[16,16,128]{2,1,0:T(8,128)(2,1)}, bf16[16,16,128]{2,1,0:T(8,128)(2,1)S(1)}, u32[]{:S(2)}, u32[]{:S(2)}) collective-permute-start(bf16[16,16,128]{2,1,0:T(8,128)(2,1)} %param.23), channel_id=1, source_target_pairs={{0,1},{1,2},{2,3},{3,4},{4,5},{5,6},{6,7},{8,9},{9,10},{10,11},{11... | collective-permute-start | bytes 196616 | tf_op jit(solution)/shard_map/ppermute | solution.py:28
  16.1 26.8 %collective-permute-start.1 = (bf16[16,16,128]{2,1,0:T(8,128)(2,1)}, bf16[16,16,128]{2,1,0:T(8,128)(2,1)S(1)}, u32[]{:S(2)}, u32[]{:S(2)}) collective-permute-start(bf16[16,16,128]{2,1,0:T(8,128)(2,1)} %param.23), channel_id=1, source_target_pairs={{1,0},{2,1},{3,2},{4,3},{5,4},{6,5},{7,6},{9,8},{10,9},{11,10},{12... | collective-permute-start | bytes 196616 | tf_op jit(solution)/shard_map/ppermute | solution.py:29
  42.9 30.8 %collective-permute-start.2 = (bf16[48,16,128]{2,1,0:T(8,128)(2,1)S(1)}, bf16[48,16,128]{2,1,0:T(8,128)(2,1)S(1)}, u32[]{:S(2)}, u32[]{:S(2)}) collective-permute-start(bf16[48,16,128]{2,1,0:T(8,128)(2,1)S(1)} %constant_dynamic-update-slice_fusion), channel_id=1, source_target_pairs={{0,8},{8,16},{16,24},{24,32},{32,40},{40,48},{48,56},{56,64},{64,7... | collective-permute-start | bytes 589832 | tf_op jit(solution)/shard_map/ppermute | solution.py:28
  46.8 26.8 %collective-permute-start.3 = (bf16[48,16,128]{2,1,0:T(8,128)(2,1)S(1)}, bf16[48,16,128]{2,1,0:T(8,128)(2,1)S(1)}, u32[]{:S(2)}, u32[]{:S(2)}) collective-permute-start(bf16[48,16,128]{2,1,0:T(8,128)(2,1)S(1)} %constant_dynamic-update-slice_fusion), channel_id=1, source_target_pairs={{8,0},{16,8},{24,16},{32,24},{40,32},{48,40},{56,48},{64,56},{72,6... | collective-permute-start | bytes 589832 | tf_op jit(solution)/shard_map/ppermute | solution.py:29
  48.9 12.0 %collective-permute-start.8 = (bf16[16,16,128]{2,1,0:T(8,128)(2,1)S(1)}, bf16[16,16,128]{2,1,0:T(8,128)(2,1)S(1)}, u32[]{:S(2)}, u32[]{:S(2)}) collective-permute-start(bf16[16,16,128]{2,1,0:T(8,128)(2,1)S(1)} %divide_convert_fusion), channel_id=1, source_target_pairs={{0,1},{1,2},{2,3},{3,4},{4,5},{5,6},{6,7},{8,9},{9,10},{10,11},{11... | collective-permute-start | bytes 196616 | tf_op jit(solution)/shard_map/ppermute | solution.py:28
  57.0 10.8 %collective-permute-start.9 = (bf16[16,16,128]{2,1,0:T(8,128)(2,1)S(1)}, bf16[16,16,128]{2,1,0:T(8,128)(2,1)S(1)}, u32[]{:S(2)}, u32[]{:S(2)}) collective-permute-start(bf16[16,16,128]{2,1,0:T(8,128)(2,1)S(1)} %divide_convert_fusion), channel_id=1, source_target_pairs={{1,0},{2,1},{3,2},{4,3},{5,4},{6,5},{7,6},{9,8},{10,9},{11,10},{12... | collective-permute-start | bytes 196616 | tf_op jit(solution)/shard_map/ppermute | solution.py:29
  60.9 13.3 %copy-start.28 = (bf16[16,16,128]{2,1,0:T(8,128)(2,1)}, bf16[16,16,128]{2,1,0:T(8,128)(2,1)S(1)}, u32[]{:S(2)}) copy-start(bf16[16,16,128]{2,1,0:T(8,128)(2,1)S(1)} %collective-permute-done.8) | copy-start | bytes 196612
  67.8 6.4 copy-start.30
  68.5 15.3 %collective-permute-start.10 = (bf16[48,16,128]{2,1,0:T(8,128)(2,1)}, bf16[48,16,128]{2,1,0:T(8,128)(2,1)}, u32[]{:S(2)}, u32[]{:S(2)}) collective-permute-start(bf16[48,16,128]{2,1,0:T(8,128)(2,1)} %pad_maximum_fusion.1), channel_id=1, source_target_pairs={{0,8},{8,16},{16,24},{24,32},{32,40},{40,48},{48,56},{56,64},{64,7... | collective-permute-start | bytes 589832 | tf_op jit(solution)/shard_map/ppermute | solution.py:28
  71.7 12.2 %collective-permute-start.11 = (bf16[48,16,128]{2,1,0:T(8,128)(2,1)}, bf16[48,16,128]{2,1,0:T(8,128)(2,1)}, u32[]{:S(2)}, u32[]{:S(2)}) collective-permute-start(bf16[48,16,128]{2,1,0:T(8,128)(2,1)} %pad_maximum_fusion.1), channel_id=1, source_target_pairs={{8,0},{16,8},{24,16},{32,24},{40,32},{48,40},{56,48},{64,56},{72,6... | collective-permute-start | bytes 589832 | tf_op jit(solution)/shard_map/ppermute | solution.py:29
  73.9 1.0 copy-start.1
  76.8 3.8 copy-start
  77.4 3.7 copy-start.13
  79.4 2.1 copy-start.7
  79.8 1.9 copy-start.9
  80.1 1.7 copy-start.11
  80.6 1.5 copy-start.32
  81.7 1.0 copy-start.5
  91.1 1.7 copy-start.12
  91.1 2.5 copy-start.10
  91.1 2.7 copy-start.8
  91.9 6.0 copy-start.14
  102.9 22.5 %copy-start.34 = (bf16[256,128]{1,0:T(8,128)(2,1)S(1)}, bf16[256,128]{1,0:T(8,128)(2,1)}, u32[]{:S(2)}) copy-start(bf16[256,128]{1,0:T(8,128)(2,1)} %convolution_convert_fusion.19) | copy-start | bytes 196612
  142.2 1.0 copy-start.3
  142.2 1.1 copy-start.4
  147.0 1.7 copy-start.16
  147.0 1.7 copy-start.17
  147.0 1.7 copy-start.18
  147.0 1.7 copy-start.19
  147.0 1.7 copy-start.20
  147.0 1.7 copy-start.21
  147.1 1.7 copy-start.22
  147.1 1.7 copy-start.23
  150.9 788.5 %all-reduce.49.cloned.1.call-start = ((), (), s32[]{:S(2)}) async-start(), calls=%async_computation.1 | async-start | bytes 4587520 | tf_op jit(solution)/shard_map/psum | solution.py:12
  694.3 16.9 %collective-permute-start.4 = (bf16[16,48,128]{2,1,0:T(8,128)(2,1)S(1)}, bf16[16,48,128]{2,1,0:T(8,128)(2,1)S(1)}, u32[]{:S(2)}, u32[]{:S(2)}) collective-permute-start(bf16[16,48,128]{2,1,0:T(8,128)(2,1)S(1)} %get-tuple-element.113), channel_id=1, source_target_pairs={{0,1},{1,2},{2,3},{3,4},{4,5},{5,6},{6,7},{8,9},{9,10},{10,11},{11... | collective-permute-start | bytes 589832 | tf_op jit(solution)/shard_map/ppermute | solution.py:18
  700.7 18.7 %collective-permute-start.5 = (bf16[16,48,128]{2,1,0:T(8,128)(2,1)S(1)}, bf16[16,48,128]{2,1,0:T(8,128)(2,1)S(1)}, u32[]{:S(2)}, u32[]{:S(2)}) collective-permute-start(bf16[16,48,128]{2,1,0:T(8,128)(2,1)S(1)} %get-tuple-element.114), channel_id=1, source_target_pairs={{1,0},{2,1},{3,2},{4,3},{5,4},{6,5},{7,6},{9,8},{10,9},{11,10},{12... | collective-permute-start | bytes 589832 | tf_op jit(solution)/shard_map/ppermute | solution.py:18
  702.0 37.2 %collective-permute-start.12 = (bf16[16,48,128]{2,1,0:T(8,128)(2,1)S(1)}, bf16[16,48,128]{2,1,0:T(8,128)(2,1)S(1)}, u32[]{:S(2)}, u32[]{:S(2)}) collective-permute-start(bf16[16,48,128]{2,1,0:T(8,128)(2,1)S(1)} %get-tuple-element.111), channel_id=1, source_target_pairs={{0,1},{1,2},{2,3},{3,4},{4,5},{5,6},{6,7},{8,9},{9,10},{10,11},{11... | collective-permute-start | bytes 589832 | tf_op jit(solution)/shard_map/ppermute | solution.py:18
  710.0 47.1 %collective-permute-start.13 = (bf16[16,48,128]{2,1,0:T(8,128)(2,1)S(1)}, bf16[16,48,128]{2,1,0:T(8,128)(2,1)S(1)}, u32[]{:S(2)}, u32[]{:S(2)}) collective-permute-start(bf16[16,48,128]{2,1,0:T(8,128)(2,1)S(1)} %get-tuple-element.112), channel_id=1, source_target_pairs={{1,0},{2,1},{3,2},{4,3},{5,4},{6,5},{7,6},{9,8},{10,9},{11,10},{12... | collective-permute-start | bytes 589832 | tf_op jit(solution)/shard_map/ppermute | solution.py:18
  719.5 55.8 %collective-permute-start.6 = (bf16[16,16,128]{2,1,0:T(8,128)(2,1)S(1)}, bf16[16,16,128]{2,1,0:T(8,128)(2,1)S(1)}, u32[]{:S(2)}, u32[]{:S(2)}) collective-permute-start(bf16[16,16,128]{2,1,0:T(8,128)(2,1)S(1)} %get-tuple-element.131), channel_id=1, source_target_pairs={{0,8},{8,16},{16,24},{24,32},{32,40},{40,48},{48,56},{56,64},{64,7... | collective-permute-start | bytes 196616 | tf_op jit(solution)/shard_map/ppermute | solution.py:18
  721.4 53.9 %collective-permute-start.7 = (bf16[16,16,128]{2,1,0:T(8,128)(2,1)S(1)}, bf16[16,16,128]{2,1,0:T(8,128)(2,1)S(1)}, u32[]{:S(2)}, u32[]{:S(2)}) collective-permute-start(bf16[16,16,128]{2,1,0:T(8,128)(2,1)S(1)} %get-tuple-element.132), channel_id=1, source_target_pairs={{8,0},{16,8},{24,16},{32,24},{40,32},{48,40},{56,48},{64,56},{72,6... | collective-permute-start | bytes 196616 | tf_op jit(solution)/shard_map/ppermute | solution.py:18
  757.1 18.9 %collective-permute-start.14 = (bf16[16,16,128]{2,1,0:T(8,128)(2,1)S(1)}, bf16[16,16,128]{2,1,0:T(8,128)(2,1)S(1)}, u32[]{:S(2)}, u32[]{:S(2)}) collective-permute-start(bf16[16,16,128]{2,1,0:T(8,128)(2,1)S(1)} %get-tuple-element.129), channel_id=1, source_target_pairs={{0,8},{8,16},{16,24},{24,32},{32,40},{40,48},{48,56},{56,64},{64,7... | collective-permute-start | bytes 196616 | tf_op jit(solution)/shard_map/ppermute | solution.py:18
  759.1 17.1 %collective-permute-start.15 = (bf16[16,16,128]{2,1,0:T(8,128)(2,1)S(1)}, bf16[16,16,128]{2,1,0:T(8,128)(2,1)S(1)}, u32[]{:S(2)}, u32[]{:S(2)}) collective-permute-start(bf16[16,16,128]{2,1,0:T(8,128)(2,1)S(1)} %get-tuple-element.130), channel_id=1, source_target_pairs={{8,0},{16,8},{24,16},{32,24},{40,32},{48,40},{56,48},{64,56},{72,6... | collective-permute-start | bytes 196616 | tf_op jit(solution)/shard_map/ppermute | solution.py:18
  939.3 2.5 copy-start.6
  941.8 1.3 copy-start.15
  (8 other events, 7.0 us)
Sparse Core Ops, SparseCore 0:
  151.0 538.3 all-reduce.46
  692.9 246.3 all-reduce.48
